TPU v7x, 256 devices: a whole 4x4x8 slice. The times are simulated.
256 devices in a mesh: req: 128 (over z, y, x), tp: 2 (over core).
Axes of the slice: x: 4, y: 4, z: 8, core: 2. Of those that a mesh axis runs over, the one named last changes fastest.
Arguments:
- stretch_states: bfloat16 [128, 128, 8192], P('req', None, 'tp'), may hold values from -6 to 6
- w_down: bfloat16 [8192, 512], P('tp'), may hold values from -0.0625 to 0.0625
- latent_gain: float32 [512], replicated, may hold values from 0.5 to 1.5
- queries: bfloat16 [128, 128, 64, 512], P('req', None, 'tp'), may hold values from -40 to 40
- page_pool: bfloat16 [128, 128, 16, 512], P('req', None, 'tp'), may hold values from -4 to 4, as said below
- page_table: int32 [128, 128], P('req'), may hold values from 0 to 127, as said below
- prefix_len: int32 [128], P('req'), may hold values from 16 to 2048, as said below
Outputs:
- new_latents: bfloat16 [128, 128, 512], P('req', 'tp')
- attended: bfloat16 [128, 128, 64, 512], P('req', None, 'tp')
Inputs may be any that keep to these rules, and one draw needn't show every extreme that they name: `prefix_len`: some request has exactly 2048 cached tokens and some exactly 16. Each row is a permutation of the devices: logical page j of request r is held by device page_table[r, j], in that device's slot r. `page_pool`: slot r of device d holds the latents of the page of request r that page_table names d.
All inputs are finite; a program needn't handle non-finite values.
Results may differ from a plain program's by a relative error of at most 0.004.
Values may be sent and summed in bfloat16 or wider, within the bound.
No kernel may reach another device: no remote copies, remote signals or barrier semaphores. Data moves between devices by JAX's collectives and lax.ppermute only.
A program may use at most 128 MiB of HBM per device.

v0:
```python
import functools

import jax
import jax.numpy as jnp
from jax import lax
from jax.experimental import pallas as pl
from jax.experimental.pallas import tpu as pltpu
from jax.sharding import PartitionSpec as P

SCORE_SCALE = 0.08838834764831845
LOG2_E = 1.4426950408889634
EXPONENT_SCALE = SCORE_SCALE * LOG2_E
MASKED = -1e30
LANES = 128
VMEM_BYTES = 26 * 2**20
SWAP = [(0, 1), (1, 0)]
ROWS = 512
FIRST_PARTS, NEXT_PARTS, LAST_PARTS = 2, 4, 2
RING = 8
PLANE = 16
STEPS = (0, 4, 1, 2, 3, -1, -2, -3)
FORWARD = {step: STEPS.index(step) for step in (1, 2, 3)}
BLOCKS = (
    (0, 0),
    *((0, 1), (1, 0), (1, 1), (-1, 1), (-1, 0)),
    *((2, 0), (2, 1), (-2, 1), (-2, 0)),
    *((3, 0), (3, 1), (4, 0), (-3, 1), (-3, 0), (4, 1)),
)
PHASES = ((0, 1), (1, 6), (6, 10), (10, 16))


def normalize(summed, latent_gain):
    mean_square = jnp.mean(summed * summed, axis=-1, keepdims=True)
    return (summed * lax.rsqrt(mean_square + 1e-06) * latent_gain).astype(jnp.bfloat16)


def product(first, second, contract):
    return lax.dot_general(
        first, second, (((1,), (contract,)), ((), ())), preferred_element_type=jnp.float32
    )


def across(column, count):
    return jnp.concatenate([column] * count, axis=1) if count > 1 else column


def lane_sums(weights):
    total = weights[:, :LANES]
    for start in range(LANES, weights.shape[1], LANES):
        total = total + weights[:, start : start + LANES]
    return total


def fill_keys(refs, takes, k_ref):
    @pl.when(pl.program_id(0) == 0)
    def _():
        start = 0
        for ref, (low, high) in zip(refs, takes):
            k_ref[pl.ds(start, high - low), :] = ref[pl.ds(low, high - low), :]
            start += high - low


def pipelined(parts, scores_of, weights_of, finish):
    scores = scores_of(0)
    pending = None
    for part in range(parts):
        following = scores_of(part + 1) if part + 1 < parts else None
        weighed = weights_of(part, scores)
        if pending is not None:
            finish(*pending)
        pending = (part, *weighed)
        scores = following
    finish(*pending)


def tile_rows(part):
    return pl.ds(part * ROWS, ROWS)


def all_rows(part, parts):
    return pl.ds(pl.multiple_of((pl.program_id(0) * parts + part) * ROWS, ROWS), ROWS)


def row_highest(scores):
    return jnp.broadcast_to(jnp.max(scores, axis=1, keepdims=True), (ROWS, LANES))


def weigh(scores, highest):
    return jnp.exp2((scores - across(highest, scores.shape[1] // LANES)) * EXPONENT_SCALE)


def first_kernel(q_ref, bias_ref, *refs, takes, parts, heads, new_rows, span):
    *key_refs, acc_ref, high_ref, sum_ref, held_ref, own_ref, mark_ref, k_ref = refs
    all_of = functools.partial(all_rows, parts=parts)
    fill_keys(key_refs, takes, k_ref)
    share = own_ref.shape[0]
    first_own = pl.multiple_of(lax.axis_index("tp") * share, share)
    own_ref[...] = key_refs[0][pl.ds(first_own, share), :]
    mark_ref[...] = jnp.zeros_like(mark_ref)

    def scores_of(part):
        q = q_ref[tile_rows(part), :]
        held_ref[all_of(part), :] = q
        scores = product(q, k_ref[...], 1)
        first_row = (pl.program_id(0) * parts + part) * ROWS
        row = first_row + lax.broadcasted_iota(jnp.int32, (ROWS, new_rows), 0)
        key = lax.broadcasted_iota(jnp.int32, (ROWS, new_rows), 1)
        fresh = jnp.where(key * heads <= row, scores[:, :new_rows], MASKED)
        return jnp.concatenate([fresh, scores[:, new_rows:] + bias_ref[:, slice(*span)]], axis=1)

    def weights_of(part, scores):
        highest = row_highest(scores)
        weights = weigh(scores, highest)
        high_ref[all_of(part), :] = highest
        sum_ref[all_of(part), :] = lane_sums(weights)
        return (weights.astype(jnp.bfloat16),)

    def finish(part, weights):
        acc_ref[all_of(part), :] = product(weights, k_ref[...], 0)

    pipelined(parts, scores_of, weights_of, finish)


def next_kernel(held_ref, bias_ref, acc_in, high_in, sum_in, *refs, takes, parts, span, last, marks):
    all_of = functools.partial(all_rows, parts=parts)
    refs = refs[marks:]
    if last:
        *key_refs, out_ref, k_ref = refs
    else:
        *key_refs, acc_ref, high_ref, sum_ref, mark_ref, k_ref = refs
        mark_ref[...] = jnp.zeros_like(mark_ref)
    fill_keys(key_refs, takes, k_ref)
    wide = k_ref.shape[1] // LANES

    def scores_of(part):
        scores = product(held_ref[all_of(part), :], k_ref[...], 1)
        return scores + bias_ref[:, slice(*span)]

    def weights_of(part, scores):
        before = high_in[all_of(part), :]
        highest = jnp.maximum(before, row_highest(scores))
        kept = jnp.exp2((before - highest) * EXPONENT_SCALE)
        weights = weigh(scores, highest)
        totals = sum_in[all_of(part), :] * kept + lane_sums(weights)
        if last:
            totals = jnp.broadcast_to(jnp.sum(totals, axis=1, keepdims=True), (ROWS, LANES))
        else:
            high_ref[all_of(part), :] = highest
            sum_ref[all_of(part), :] = totals
        return weights.astype(jnp.bfloat16), kept, totals

    def finish(part, weights, kept, totals):
        accumulated = acc_in[all_of(part), :] * across(kept, wide)
        accumulated = accumulated + product(weights, k_ref[...], 0)
        if last:
            share = across(1.0 / totals, wide)
            out_ref[tile_rows(part), :] = (accumulated * share).astype(jnp.bfloat16)
        else:
            acc_ref[all_of(part), :] = accumulated

    pipelined(parts, scores_of, weights_of, finish)


def sort_kernel(pool_ref, out_ref, sems):
    height = lax.axis_index("req") // PLANE
    sign = 1 - 2 * lax.axis_index("tp")
    moves = []
    for number, step in enumerate(STEPS):
        source = pool_ref.at[lax.rem(height + sign * step + RING, RING)]
        moves.append(pltpu.make_async_copy(source, out_ref.at[:, number], sems.at[number]))
    for move in moves:
        move.start()
    for move in moves:
        move.wait()


def whole(array):
    return pl.BlockSpec(array.shape, lambda i: (0,) * array.ndim)


def resident(array):
    return pltpu.with_memory_space_constraint(array, pltpu.VMEM)


RESIDENT = pl.BlockSpec(memory_space=pltpu.VMEM)


def sort_pages(pool):
    ring, plane, half_rows, width = pool.shape
    return pl.pallas_call(
        sort_kernel,
        in_specs=[pl.BlockSpec(memory_space=pl.ANY)],
        out_specs=RESIDENT,
        out_shape=pltpu.VMEM((plane, ring, half_rows, width), pool.dtype),
        scratch_shapes=[pltpu.SemaphoreType.DMA((ring,))],
        compiler_params=pltpu.CompilerParams(vmem_limit_bytes=VMEM_BYTES),
        name="sort_pages",
    )(pltpu.with_memory_space_constraint(pool, pltpu.HBM))


def attend(kernel, flat_q, keys, bias, state, mark, parts, out_specs, out_shape, aliases):
    rows, width = flat_q.shape
    takes = [(key[1:] if isinstance(key, tuple) else (0, key.shape[0])) for key in keys]
    keys = [key[0] if isinstance(key, tuple) else key for key in keys]
    key_count = sum(high - low for low, high in takes)
    q_spec = RESIDENT if state else row_tile(parts, width)
    q_space = pltpu.VMEM if state else pltpu.HBM
    return pl.pallas_call(
        functools.partial(kernel, takes=takes, parts=parts),
        grid=(rows // (ROWS * parts),),
        in_specs=[q_spec, whole(bias)]
        + [RESIDENT for _ in state]
        + [whole(part) for part in mark]
        + [RESIDENT for _ in keys],
        out_specs=out_specs,
        out_shape=out_shape,
        input_output_aliases=aliases,
        scratch_shapes=[pltpu.VMEM((key_count, width), jnp.bfloat16)],
        compiler_params=pltpu.CompilerParams(vmem_limit_bytes=VMEM_BYTES),
        cost_estimate=pl.CostEstimate(flops=0, bytes_accessed=1 << 16, transcendentals=0),
        name="attend",
    )(
        pltpu.with_memory_space_constraint(flat_q, q_space),
        bias,
        *[resident(part) for part in state],
        *mark,
        *[resident(key) for key in keys],
    )


def row_tile(parts, width):
    return pl.BlockSpec((ROWS * parts, width), lambda i: (i, 0))


def state_shapes(rows, width):
    shapes = [(rows, width), (rows, LANES), (rows, LANES)]
    return [pltpu.VMEM(shape, jnp.float32) for shape in shapes]


def attend_first(flat_q, keys, bias, span, heads):
    rows, width = flat_q.shape
    new_rows = keys[0].shape[0]
    small = [(new_rows // 2, width), (8, LANES)]
    return attend(
        functools.partial(first_kernel, heads=heads, new_rows=new_rows, span=span),
        flat_q,
        keys,
        bias,
        [],
        [],
        FIRST_PARTS,
        [RESIDENT] * 4 + [pl.BlockSpec(shape, lambda i: (0, 0)) for shape in small],
        state_shapes(rows, width)
        + [
            pltpu.VMEM((rows, width), jnp.bfloat16),
            jax.ShapeDtypeStruct(small[0], jnp.bfloat16),
            jax.ShapeDtypeStruct(small[1], jnp.float32),
        ],
        {},
    )


def attend_next(held, keys, bias, span, state, mark, last):
    rows, width = held.shape
    kernel = functools.partial(next_kernel, span=span, last=last, marks=len(mark))
    if last:
        out = row_tile(LAST_PARTS, width), jax.ShapeDtypeStruct((rows, width), jnp.bfloat16)
        return attend(kernel, held, keys, bias, state, mark, LAST_PARTS, *out, {})
    specs = [RESIDENT] * 3 + [pl.BlockSpec((8, LANES), lambda i: (0, 0))]
    shapes = state_shapes(rows, width) + [jax.ShapeDtypeStruct((8, LANES), jnp.float32)]
    aliases = {2: 0, 3: 1, 4: 2}
    return attend(kernel, held, keys, bias, state, mark, NEXT_PARTS, specs, shapes, aliases)


def along_ring(blocks, step):
    pairs = []
    for z in range(RING):
        for place in range(PLANE):
            for core, distance in ((0, step), (1, -step)):
                target = ((z + distance) % RING) * PLANE + place
                pairs.append(((z * PLANE + place) * 2 + core, target * 2 + core))
    return lax.ppermute(blocks, ("req", "tp"), pairs)


def body(stretch_states, w_down, latent_gain, queries, page_pool, page_table, prefix_len):
    side = lax.axis_index("tp")
    sign = 1 - 2 * side
    height = lax.axis_index("req") // PLANE
    half_rows, width = page_pool.shape[2:]
    pool = page_pool[0].reshape(RING, PLANE, half_rows, width)

    by_place = sort_pages(pool)
    by_place, page_table, stretch_states = lax.optimization_barrier(
        (by_place, page_table, stretch_states)
    )
    planes = [[z * PLANE + place for place in range(PLANE)] for z in range(RING)]
    crossed = lax.all_to_all(
        by_place, "req", split_axis=0, concat_axis=0, axis_index_groups=planes, tiled=True
    )
    partial_value = jnp.dot(stretch_states[0], w_down, preferred_element_type=jnp.float32)
    summed = partial_value + lax.ppermute(partial_value, "tp", SWAP)
    latents = normalize(summed, latent_gain)
    new_rows = latents.shape[0]

    place = jnp.arange(RING * PLANE, dtype=jnp.int32)
    logical = jnp.sum(
        jnp.where(page_table[0][None, :] == place[:, None], place[None, :], 0), axis=1
    ).reshape(RING, PLANE)
    steps = jnp.array([step for step, _ in BLOCKS], dtype=jnp.int32)
    others = jnp.array([other for _, other in BLOCKS], dtype=jnp.int32)
    page = jnp.take(logical, (height - sign * steps) % RING, axis=0)
    half = (side + others) % 2
    token = page[:, :, None] * (2 * half_rows) + (half * half_rows)[:, None, None]
    token = token + jnp.arange(half_rows, dtype=jnp.int32)
    bias = jnp.where(token.reshape(1, -1) < prefix_len[0], 0.0, MASKED).astype(jnp.float32)

    crossed, latents, bias = lax.optimization_barrier((crossed, latents, bias))
    handed = lax.ppermute(
        jnp.stack([crossed[:, 5], crossed[:, 6], crossed[:, 7], crossed[:, 0]]), "tp", SWAP
    )
    heads = queries.shape[2]
    flat_q = queries[0].reshape(new_rows * heads, width)
    span = lambda phase: tuple(edge * PLANE * half_rows for edge in PHASES[phase])
    block_rows = PLANE * half_rows
    flat = lambda block: block.reshape(-1, width)
    both = lambda block: [flat(block), flat(lax.ppermute(block, "tp", SWAP))]

    one = along_ring(jnp.stack([crossed[:, FORWARD[1]], handed[0], crossed[:, 1]]), 1)
    two = along_ring(jnp.stack([crossed[:, FORWARD[2]], handed[1]]), 2)
    keys = [latents, flat(crossed[:, 0])]
    *state, held, own_rows, mark = attend_first(flat_q, keys, bias, span(0), heads)

    one, mark = lax.optimization_barrier((one, mark))
    three = along_ring(jnp.stack([crossed[:, FORWARD[3]], handed[2], one[2]]), 3)
    keys = [(flat(handed), 3 * block_rows, 4 * block_rows)]
    keys += [(key, 0, 2 * block_rows) for key in both(one)]
    *state, mark = attend_next(held, keys, bias, span(1), state, [mark], False)
    two, mark = lax.optimization_barrier((two, mark))
    *state, mark = attend_next(held, both(two), bias, span(2), state, [mark], False)
    three, mark = lax.optimization_barrier((three, mark))
    attended = attend_next(held, both(three), bias, span(3), state, [mark], True)
    return (own_rows[None], attended.reshape(1, new_rows, heads, width))


def solution(mesh):
    return jax.shard_map(
        body,
        mesh=mesh,
        in_specs=(
            P("req", None, "tp"),
            P("tp", None),
            P(),
            P("req", None, "tp", None),
            P("req", None, "tp", None),
            P("req", None),
            P("req"),
        ),
        out_specs=(P("req", "tp", None), P("req", None, "tp", None)),
        check_vma=False,
    )
```

profile of v0, /device:TPU:1, one launch (start us, length us, event | category | flops | bytes accessed | tf_op | source)
XLA Modules:
  0.0 76.4 jit_solution(9967889856719065934)
XLA Ops:
  0.6 0.0 copy-start
  0.6 2.4 %sort_pages.1 = bf16[16,8,8,512]{3,2,1,0:T(8,128)(2,1)} custom-call(bf16[8,16,8,512]{3,2,1,0:T(8,128)(2,1)} %bitcast.45), custom_call_target="tpu_custom_call" | custom-call | tf_op jit(solution)/shard_map/sort_pages/pallas_call | solution.py:190
  3.1 0.0 copy-start.4
  3.1 0.0 copy-start.2
  3.1 0.0 copy-start.3
  3.1 0.0 copy-start.1
  3.1 7.7 %all-to-all-start = ((bf16[16,8,8,512]{3,2,1,0:T(8,128)(2,1)}), bf16[16,8,8,512]{3,2,1,0:T(8,128)(2,1)S(1)}, u32[]{:S(2)}, u32[]{:S(2)}) async-start(bf16[16,8,8,512]{3,2,1,0:T(8,128)(2,1)} %sort_pages.1), calls=%async_computation | async-start | bytes 2097152 | tf_op jit(solution)/shard_map/all_to_all | solution.py:297
  10.9 0.0 copy-done
  10.9 2.9 %fusion = f32[128,512]{1,0:T(8,128)S(1)} fusion(bf16[4096,512]{1,0:T(8,128)(2,1)} %param.10, bf16[1,128,4096]{2,1,0:T(8,128)(2,1)S(1)} %copy-done), kind=kOutput, calls=%fused_computation.1 | convolution fusion | flops 536870912 | bytes 5505024 | tf_op jit(solution)/shard_map/dot_general | solution.py:300
  13.8 1.0 %collective-permute-start = (f32[128,512]{1,0:T(8,128)S(1)}, f32[128,512]{1,0:T(8,128)S(1)}, u32[]{:S(2)}, u32[]{:S(2)}) collective-permute-start(f32[128,512]{1,0:T(8,128)S(1)} %fusion), channel_id=1, source_target_pairs={{0,1},{1,0},{2,3},{3,2},{4,5},{5,4},{6,7},{7,6},{8,9},{9,8},{10,11... | collective-permute-start | bytes 786440 | tf_op jit(solution)/shard_map/ppermute | solution.py:301
  14.8 0.0 copy-done.4
  14.8 0.0 copy-done.2
  14.9 0.0 copy-done.3
  14.9 0.1 select_reduce_fusion
  15.0 0.1 reshape.118
  15.1 0.6 gather_fusion
  15.7 0.1 multiply_add_fusion
  16.4 0.1 fusion.2
  16.5 0.1 select_n.54.bias_ref
  16.6 0.0 collective-permute-done
  16.6 0.1 multiply_reduce_fusion
  16.8 0.0 copy-done.1
  16.8 0.1 multiply_convert_fusion.refs_0_
  16.9 10.0 %all-to-all-done = bf16[16,8,8,512]{3,2,1,0:T(8,128)(2,1)S(1)} async-done(((bf16[16,8,8,512]{3,2,1,0:T(8,128)(2,1)}), bf16[16,8,8,512]{3,2,1,0:T(8,128)(2,1)S(1)}, u32[]{:S(2)}, u32[]{:S(2)}) %all-to-all-start) | async-done | bytes 1048608 | tf_op jit(solution)/shard_map/all_to_all | solution.py:297
  26.8 0.1 slice_bitcast_fusion
  26.9 0.1 pad_maximum_fusion
  27.0 2.7 %collective-permute-start.1 = (bf16[4,16,8,512]{3,2,1,0:T(8,128)(2,1)S(1)}, bf16[4,16,8,512]{3,2,1,0:T(8,128)(2,1)S(1)}, u32[]{:S(2)}, u32[]{:S(2)}) collective-permute-start(bf16[4,16,8,512]{3,2,1,0:T(8,128)(2,1)S(1)} %pad_maximum_fusion), channel_id=1, source_target_pairs={{0,1},{1,0},{2,3},{3,2},{4,5},{5,4},{6,7},{7,6},{8,9},{9,8},{10,11... | collective-permute-start | bytes 1572872 | tf_op jit(solution)/shard_map/ppermute | solution.py:318
  29.7 1.5 %collective-permute-done.1 = bf16[4,16,8,512]{3,2,1,0:T(8,128)(2,1)S(1)} collective-permute-done((bf16[4,16,8,512]{3,2,1,0:T(8,128)(2,1)S(1)}, bf16[4,16,8,512]{3,2,1,0:T(8,128)(2,1)S(1)}, u32[]{:S(2)}, u32[]{:S(2)}) %collective-permute-start.1) | collective-permute-done | bytes 524320 | tf_op jit(solution)/shard_map/ppermute | solution.py:318
  31.3 5.7 %collective-permute-start.2 = (bf16[3,16,8,512]{3,2,1,0:T(8,128)(2,1)S(1)}, bf16[3,16,8,512]{3,2,1,0:T(8,128)(2,1)S(1)}, u32[]{:S(2)}, u32[]{:S(2)}) collective-permute-start(bf16[3,16,8,512]{3,2,1,0:T(8,128)(2,1)S(1)} %pad_maximum_fusion.1), channel_id=1, source_target_pairs={{0,32},{1,225},{2,34},{3,227},{4,36},{5,229},{6,38},{7,231},{8,40}... | collective-permute-start | bytes 1179656 | tf_op jit(solution)/shard_map/ppermute | solution.py:282
  37.0 5.7 %attend.4 = (f32[4096,512]{1,0:T(8,128)S(1)}, f32[4096,128]{1,0:T(8,128)S(1)}, f32[4096,128]{1,0:T(8,128)S(1)}, bf16[4096,512]{1,0:T(8,128)(2,1)S(1)}, bf16[64,512]{1,0:T(8,128)(2,1)}, /*index=5*/f32[8,128]{1,0:T(8,128)S(1)}) custom-call(bf16[4096,512]{1,0:T(8,128)(2,1)} %bitcast.43, f32[1,2048]{1,0:T(1,128)S(1)} %select_n.54.bias_ref, ...), custom_call_target="tpu_custom_call" | custom-call | bytes 65536 | tf_op jit(solution)/shard_map/attend/pallas_call | solution.py:208
  42.7 1.2 %collective-permute-start.4 = (bf16[2,16,8,512]{3,2,1,0:T(8,128)(2,1)S(1)}, bf16[2,16,8,512]{3,2,1,0:T(8,128)(2,1)S(1)}, u32[]{:S(2)}, u32[]{:S(2)}) collective-permute-start(bf16[2,16,8,512]{3,2,1,0:T(8,128)(2,1)S(1)} %pad_maximum_fusion.3), channel_id=1, source_target_pairs={{0,64},{1,193},{2,66},{3,195},{4,68},{5,197},{6,70},{7,199},{8,72}... | collective-permute-start | bytes 786440 | tf_op jit(solution)/shard_map/ppermute | solution.py:282
  44.0 0.0 collective-permute-done.2
  44.0 0.0 collective-permute-start.3
  44.1 2.1 %collective-permute-start.6 = (bf16[3,16,8,512]{3,2,1,0:T(8,128)(2,1)S(1)}, bf16[3,16,8,512]{3,2,1,0:T(8,128)(2,1)S(1)}, u32[]{:S(2)}, u32[]{:S(2)}) collective-permute-start(bf16[3,16,8,512]{3,2,1,0:T(8,128)(2,1)S(1)} %pad_maximum_fusion.2), channel_id=1, source_target_pairs={{0,96},{1,161},{2,98},{3,163},{4,100},{5,165},{6,102},{7,167},{8,1... | collective-permute-start | bytes 1179656 | tf_op jit(solution)/shard_map/ppermute | solution.py:282
  46.2 0.0 collective-permute-done.3
  46.2 8.1 %attend.5 = (f32[4096,512]{1,0:T(8,128)S(1)}, f32[4096,128]{1,0:T(8,128)S(1)}, f32[4096,128]{1,0:T(8,128)S(1)}, f32[8,128]{1,0:T(8,128)S(1)}) custom-call(bf16[4096,512]{1,0:T(8,128)(2,1)S(1)} %get-tuple-element.35.held_ref, f32[1,2048]{1,0:T(1,128)S(1)} %select_n.54.bias_ref, ...), custom_call_target="tpu_custom_call", output_to_operand_aliasing={{0}: (2, {}), {1}: (3, {}), {2}: (4, {})} | custom-call | bytes 65536 | tf_op jit(solution)/shard_map/attend/pallas_call | solution.py:208
  54.3 0.0 collective-permute-done.4
  54.3 1.1 %collective-permute-start.5 = (bf16[2,16,8,512]{3,2,1,0:T(8,128)(2,1)S(1)}, bf16[2,16,8,512]{3,2,1,0:T(8,128)(2,1)S(1)}, u32[]{:S(2)}, u32[]{:S(2)}) collective-permute-start(bf16[2,16,8,512]{3,2,1,0:T(8,128)(2,1)S(1)} %collective-permute-done.4), channel_id=1, source_target_pairs={{0,1},{1,0},{2,3},{3,2},{4,5},{5,4},{6,7},{7,6},{8,9},{9,8},{10,11... | collective-permute-start | bytes 786440 | tf_op jit(solution)/shard_map/ppermute | solution.py:326
  55.3 1.2 %collective-permute-done.5 = bf16[2,16,8,512]{3,2,1,0:T(8,128)(2,1)S(1)} collective-permute-done((bf16[2,16,8,512]{3,2,1,0:T(8,128)(2,1)S(1)}, bf16[2,16,8,512]{3,2,1,0:T(8,128)(2,1)S(1)}, u32[]{:S(2)}, u32[]{:S(2)}) %collective-permute-start.5) | collective-permute-done | bytes 262176 | tf_op jit(solution)/shard_map/ppermute | solution.py:326
  56.5 5.6 %attend.6 = (f32[4096,512]{1,0:T(8,128)S(1)}, f32[4096,128]{1,0:T(8,128)S(1)}, f32[4096,128]{1,0:T(8,128)S(1)}, f32[8,128]{1,0:T(8,128)S(1)}) custom-call(bf16[4096,512]{1,0:T(8,128)(2,1)S(1)} %get-tuple-element.35.held_ref, f32[1,2048]{1,0:T(1,128)S(1)} %select_n.54.bias_ref, ...), custom_call_target="tpu_custom_call", output_to_operand_aliasing={{0}: (2, {}), {1}: (3, {}), {2}: (4, {})} | custom-call | bytes 65536 | tf_op jit(solution)/shard_map/attend/pallas_call | solution.py:208
  62.1 0.0 collective-permute-done.6
  62.1 3.6 %collective-permute-start.7 = (bf16[3,16,8,512]{3,2,1,0:T(8,128)(2,1)S(1)}, bf16[3,16,8,512]{3,2,1,0:T(8,128)(2,1)S(1)}, u32[]{:S(2)}, u32[]{:S(2)}) collective-permute-start(bf16[3,16,8,512]{3,2,1,0:T(8,128)(2,1)S(1)} %collective-permute-done.6), channel_id=1, source_target_pairs={{0,1},{1,0},{2,3},{3,2},{4,5},{5,4},{6,7},{7,6},{8,9},{9,8},{10,11... | collective-permute-start | bytes 1179656 | tf_op jit(solution)/shard_map/ppermute | solution.py:326
  65.7 1.3 %collective-permute-done.7 = bf16[3,16,8,512]{3,2,1,0:T(8,128)(2,1)S(1)} collective-permute-done((bf16[3,16,8,512]{3,2,1,0:T(8,128)(2,1)S(1)}, bf16[3,16,8,512]{3,2,1,0:T(8,128)(2,1)S(1)}, u32[]{:S(2)}, u32[]{:S(2)}) %collective-permute-start.7) | collective-permute-done | bytes 393248 | tf_op jit(solution)/shard_map/ppermute | solution.py:326
  67.1 9.4 %attend.7 = bf16[4096,512]{1,0:T(8,128)(2,1)} custom-call(bf16[4096,512]{1,0:T(8,128)(2,1)S(1)} %get-tuple-element.35.held_ref, f32[1,2048]{1,0:T(1,128)S(1)} %select_n.54.bias_ref, f32[4096,512]{1,0:T(8,128)S(1)} %get-tuple-element.48.acc_in, f32[4096,128]{1,0:T(8,128)S(1)} %get-tuple-element.49.high_in, f32[4096,128]{1,0:T(8,128)S(1)} %get-tuple-element.50.sum_in, ...), custom_call_target="tpu_custom_call" | custom-call | bytes 65536 | tf_op jit(solution)/shard_map/attend/pallas_call | solution.py:208
  (10 shorter events, 0.2 us)
Async XLA Ops:
  0.6 10.2 %copy-start = (bf16[1,128,4096]{2,1,0:T(8,128)(2,1)S(1)}, bf16[1,128,4096]{2,1,0:T(8,128)(2,1)}, u32[]{:S(2)}) copy-start(bf16[1,128,4096]{2,1,0:T(8,128)(2,1)} %param.9) | copy-start | bytes 3145732
  3.1 11.8 %copy-start.4 = (s32[16]{0:T(128)S(1)}, s32[16]{0:T(128)}, u32[]{:S(2)}) copy-start(s32[16]{0:T(128)} %constant.80.clone) | copy-start | bytes 196
  3.1 11.8 %copy-start.2 = (s32[16]{0:T(128)S(1)}, s32[16]{0:T(128)}, u32[]{:S(2)}) copy-start(s32[16]{0:T(128)} %constant.79.clone) | copy-start | bytes 196
  3.1 11.8 %copy-start.3 = (s32[1,128]{1,0:T(1,128)S(1)}, s32[1,128]{1,0:T(1,128)}, u32[]{:S(2)}) copy-start(s32[1,128]{1,0:T(1,128)} %param.14) | copy-start | bytes 1540
  3.1 13.6 %copy-start.1 = (f32[512]{0:T(512)S(1)}, f32[512]{0:T(512)}, u32[]{:S(2)}) copy-start(f32[512]{0:T(512)} %param.11) | copy-start | bytes 6148
  3.1 23.7 %all-to-all-start = ((bf16[16,8,8,512]{3,2,1,0:T(8,128)(2,1)}), bf16[16,8,8,512]{3,2,1,0:T(8,128)(2,1)S(1)}, u32[]{:S(2)}, u32[]{:S(2)}) async-start(bf16[16,8,8,512]{3,2,1,0:T(8,128)(2,1)} %sort_pages.1), calls=%async_computation | async-start | bytes 2097152 | tf_op jit(solution)/shard_map/all_to_all | solution.py:297
  13.8 2.8 %collective-permute-start = (f32[128,512]{1,0:T(8,128)S(1)}, f32[128,512]{1,0:T(8,128)S(1)}, u32[]{:S(2)}, u32[]{:S(2)}) collective-permute-start(f32[128,512]{1,0:T(8,128)S(1)} %fusion), channel_id=1, source_target_pairs={{0,1},{1,0},{2,3},{3,2},{4,5},{5,4},{6,7},{7,6},{8,9},{9,8},{10,11... | collective-permute-start | bytes 786440 | tf_op jit(solution)/shard_map/ppermute | solution.py:301
  27.0 4.2 %collective-permute-start.1 = (bf16[4,16,8,512]{3,2,1,0:T(8,128)(2,1)S(1)}, bf16[4,16,8,512]{3,2,1,0:T(8,128)(2,1)S(1)}, u32[]{:S(2)}, u32[]{:S(2)}) collective-permute-start(bf16[4,16,8,512]{3,2,1,0:T(8,128)(2,1)S(1)} %pad_maximum_fusion), channel_id=1, source_target_pairs={{0,1},{1,0},{2,3},{3,2},{4,5},{5,4},{6,7},{7,6},{8,9},{9,8},{10,11... | collective-permute-start | bytes 1572872 | tf_op jit(solution)/shard_map/ppermute | solution.py:318
  31.3 12.7 %collective-permute-start.2 = (bf16[3,16,8,512]{3,2,1,0:T(8,128)(2,1)S(1)}, bf16[3,16,8,512]{3,2,1,0:T(8,128)(2,1)S(1)}, u32[]{:S(2)}, u32[]{:S(2)}) collective-permute-start(bf16[3,16,8,512]{3,2,1,0:T(8,128)(2,1)S(1)} %pad_maximum_fusion.1), channel_id=1, source_target_pairs={{0,32},{1,225},{2,34},{3,227},{4,36},{5,229},{6,38},{7,231},{8,40}... | collective-permute-start | bytes 1179656 | tf_op jit(solution)/shard_map/ppermute | solution.py:282
  42.7 11.5 %collective-permute-start.4 = (bf16[2,16,8,512]{3,2,1,0:T(8,128)(2,1)S(1)}, bf16[2,16,8,512]{3,2,1,0:T(8,128)(2,1)S(1)}, u32[]{:S(2)}, u32[]{:S(2)}) collective-permute-start(bf16[2,16,8,512]{3,2,1,0:T(8,128)(2,1)S(1)} %pad_maximum_fusion.3), channel_id=1, source_target_pairs={{0,64},{1,193},{2,66},{3,195},{4,68},{5,197},{6,70},{7,199},{8,72}... | collective-permute-start | bytes 786440 | tf_op jit(solution)/shard_map/ppermute | solution.py:282
  44.0 2.2 %collective-permute-start.3 = (bf16[3,16,8,512]{3,2,1,0:T(8,128)(2,1)S(1)}, bf16[3,16,8,512]{3,2,1,0:T(8,128)(2,1)S(1)}, u32[]{:S(2)}, u32[]{:S(2)}) collective-permute-start(bf16[3,16,8,512]{3,2,1,0:T(8,128)(2,1)S(1)} %collective-permute-done.2), channel_id=1, source_target_pairs={{0,1},{1,0},{2,3},{3,2},{4,5},{5,4},{6,7},{7,6},{8,9},{9,8},{10,11... | collective-permute-start | bytes 1179656 | tf_op jit(solution)/shard_map/ppermute | solution.py:326
  44.1 18.0 %collective-permute-start.6 = (bf16[3,16,8,512]{3,2,1,0:T(8,128)(2,1)S(1)}, bf16[3,16,8,512]{3,2,1,0:T(8,128)(2,1)S(1)}, u32[]{:S(2)}, u32[]{:S(2)}) collective-permute-start(bf16[3,16,8,512]{3,2,1,0:T(8,128)(2,1)S(1)} %pad_maximum_fusion.2), channel_id=1, source_target_pairs={{0,96},{1,161},{2,98},{3,163},{4,100},{5,165},{6,102},{7,167},{8,1... | collective-permute-start | bytes 1179656 | tf_op jit(solution)/shard_map/ppermute | solution.py:282
  54.3 2.2 %collective-permute-start.5 = (bf16[2,16,8,512]{3,2,1,0:T(8,128)(2,1)S(1)}, bf16[2,16,8,512]{3,2,1,0:T(8,128)(2,1)S(1)}, u32[]{:S(2)}, u32[]{:S(2)}) collective-permute-start(bf16[2,16,8,512]{3,2,1,0:T(8,128)(2,1)S(1)} %collective-permute-done.4), channel_id=1, source_target_pairs={{0,1},{1,0},{2,3},{3,2},{4,5},{5,4},{6,7},{7,6},{8,9},{9,8},{10,11... | collective-permute-start | bytes 786440 | tf_op jit(solution)/shard_map/ppermute | solution.py:326
  62.1 5.0 %collective-permute-start.7 = (bf16[3,16,8,512]{3,2,1,0:T(8,128)(2,1)S(1)}, bf16[3,16,8,512]{3,2,1,0:T(8,128)(2,1)S(1)}, u32[]{:S(2)}, u32[]{:S(2)}) collective-permute-start(bf16[3,16,8,512]{3,2,1,0:T(8,128)(2,1)S(1)} %collective-permute-done.6), channel_id=1, source_target_pairs={{0,1},{1,0},{2,3},{3,2},{4,5},{5,4},{6,7},{7,6},{8,9},{9,8},{10,11... | collective-permute-start | bytes 1179656 | tf_op jit(solution)/shard_map/ppermute | solution.py:326
where the time goes:
time: 76.7 us; the launch traced here: 76.4 us
  Pallas kernels  31.1 us (41%)
  starting transfers between devices  25.2 us (33%)
  waiting for transfers between devices  14 us (18%)
  matrix products  2.9 us (4%)
  between operations  1.53 us (2%)
  local copies, waits for them, and re-layouts  0.92 us (1%)
    pallas_call x4, Pallas kernels, attend(): pl.pallas_call(functools.partial(kernel, takes=takes, parts=parts), grid=...  28.7 us
    all_to_all x1, waiting for transfers between devices, body(): lax.all_to_all(by_place, 'req', split_axis=0, concat_axis=0, axis_index_g...  9.98 us
    ppermute x3, starting transfers between devices, along_ring(): return lax.ppermute(blocks, ('req', 'tp'), pairs)  9.01 us
    all_to_all x1, starting transfers between devices, body(): lax.all_to_all(by_place, 'req', split_axis=0, concat_axis=0, axis_index_g...  7.73 us
    ppermute x3, starting transfers between devices, body(): both = lambda block: [flat(block), flat(lax.ppermute(block, 'tp', SWAP))]  4.7 us
    dot_general x1, matrix products, body(): jnp.dot(stretch_states[0], w_down, preferred_element_type=jnp.float32)  2.9 us
    ppermute x1, starting transfers between devices, body(): lax.ppermute(jnp.stack([crossed[:, 5], crossed[:, 6], crossed[:, 7], cros...  2.7 us
    ppermute x3, waiting for transfers between devices, body(): both = lambda block: [flat(block), flat(lax.ppermute(block, 'tp', SWAP))]  2.51 us
  transfers between devices with their start and end apart: 9, of which 4 were waited for; matrix products, arithmetic and copies ran while one was open for 6% of the time, Pallas kernels for 25%

commit v1 on v0

--- a/solution.py
+++ b/solution.py
@@ -12,10 +12,10 @@
 EXPONENT_SCALE = SCORE_SCALE * LOG2_E
 MASKED = -1e30
 LANES = 128
-VMEM_BYTES = 26 * 2**20
+VMEM_BYTES = 30 * 2**20
 SWAP = [(0, 1), (1, 0)]
 ROWS = 512
-FIRST_PARTS, NEXT_PARTS, LAST_PARTS = 2, 4, 2
+FIRST_PARTS, NEXT_PARTS, LAST_PARTS = 4, 4, 2
 RING = 8
 PLANE = 16
 STEPS = (0, 4, 1, 2, 3, -1, -2, -3)
@@ -26,7 +26,7 @@
     *((2, 0), (2, 1), (-2, 1), (-2, 0)),
     *((3, 0), (3, 1), (4, 0), (-3, 1), (-3, 0), (4, 1)),
 )
-PHASES = ((0, 1), (1, 6), (6, 10), (10, 16))
+PHASES = ((0, 2), (2, 6), (6, 10), (10, 16))
 
 
 def normalize(summed, latent_gain):
@@ -327,16 +327,16 @@
 
     one = along_ring(jnp.stack([crossed[:, FORWARD[1]], handed[0], crossed[:, 1]]), 1)
     two = along_ring(jnp.stack([crossed[:, FORWARD[2]], handed[1]]), 2)
-    keys = [latents, flat(crossed[:, 0])]
+    keys = [latents, flat(crossed[:, 0]), (flat(handed), 3 * block_rows, 4 * block_rows)]
     *state, held, own_rows, mark = attend_first(flat_q, keys, bias, span(0), heads)
 
     one, mark = lax.optimization_barrier((one, mark))
     three = along_ring(jnp.stack([crossed[:, FORWARD[3]], handed[2], one[2]]), 3)
-    keys = [(flat(handed), 3 * block_rows, 4 * block_rows)]
-    keys += [(key, 0, 2 * block_rows) for key in both(one)]
+    two, mark = lax.optimization_barrier((two, mark))
+    two = both(two)
+    keys = [(key, 0, 2 * block_rows) for key in both(one)]
     *state, mark = attend_next(held, keys, bias, span(1), state, [mark], False)
-    two, mark = lax.optimization_barrier((two, mark))
-    *state, mark = attend_next(held, both(two), bias, span(2), state, [mark], False)
+    *state, mark = attend_next(held, two, bias, span(2), state, [mark], False)
     three, mark = lax.optimization_barrier((three, mark))
     attended = attend_next(held, both(three), bias, span(3), state, [mark], True)
     return (own_rows[None], attended.reshape(1, new_rows, heads, width))

time: 76.7 us -> 76.5 us (level)
  starting transfers between devices: 25.2 us -> 27 us
  waiting for transfers between devices: 14 us -> 12.9 us
  Pallas kernels: 31.1 us -> 30.3 us
    ppermute x3, starting transfers between devices: 4.7 us -> 7.03 us  [body(): both = lambda block: [flat(block), flat(lax.ppermute(block, 'tp', SWAP))]]
    ppermute x3, waiting for transfers between devices: 2.51 us -> 1.35 us  [body(): both = lambda block: [flat(block), flat(lax.ppermute(block, 'tp', SWAP))]]
    pallas_call x4, Pallas kernels: 28.7 us -> 27.9 us  [attend(): pl.pallas_call(functools.partial(kernel, takes=takes, parts=parts), grid=...]
  transfers between devices with their start and end apart: 9 -> 9, of which waited for: 4 -> 3; matrix products, arithmetic and copies ran while one was open for 6% -> 6% of each run, Pallas kernels for 25% -> 24%
where the time goes in v1:
time: 76.5 us; the launch traced here: 76.3 us
  Pallas kernels  30.3 us (40%)
  starting transfers between devices  27 us (35%)
  waiting for transfers between devices  12.9 us (17%)
  matrix products  2.9 us (4%)
  between operations  1.53 us (2%)
  local copies, waits for them, and re-layouts  0.93 us (1%)
    pallas_call x4, Pallas kernels, attend(): pl.pallas_call(functools.partial(kernel, takes=takes, parts=parts), grid=...  27.9 us
    all_to_all x1, waiting for transfers between devices, body(): lax.all_to_all(by_place, 'req', split_axis=0, concat_axis=0, axis_index_g...  9.98 us
    ppermute x3, starting transfers between devices, along_ring(): return lax.ppermute(blocks, ('req', 'tp'), pairs)  8.54 us
    all_to_all x1, starting transfers between devices, body(): lax.all_to_all(by_place, 'req', split_axis=0, concat_axis=0, axis_index_g...  7.73 us
    ppermute x3, starting transfers between devices, body(): both = lambda block: [flat(block), flat(lax.ppermute(block, 'tp', SWAP))]  7.03 us
    dot_general x1, matrix products, body(): jnp.dot(stretch_states[0], w_down, preferred_element_type=jnp.float32)  2.9 us
    ppermute x1, starting transfers between devices, body(): lax.ppermute(jnp.stack([crossed[:, 5], crossed[:, 6], crossed[:, 7], cros...  2.7 us
    pallas_call x1, Pallas kernels, sort_pages(): pl.pallas_call(sort_kernel, in_specs=[pl.BlockSpec(memory_space=pl.ANY)],...  2.41 us
  transfers between devices with their start and end apart: 9, of which 3 were waited for; matrix products, arithmetic and copies ran while one was open for 6% of the time, Pallas kernels for 24%

profile of v1, /device:TPU:1, one launch (start us, length us, event | category | flops | bytes accessed | tf_op | source)
XLA Modules:
  0.0 76.3 jit_solution(15981208691565112380)
XLA Ops:
  0.6 0.0 copy-start
  0.6 2.4 %sort_pages.1 = bf16[16,8,8,512]{3,2,1,0:T(8,128)(2,1)} custom-call(bf16[8,16,8,512]{3,2,1,0:T(8,128)(2,1)} %bitcast.45), custom_call_target="tpu_custom_call" | custom-call | tf_op jit(solution)/shard_map/sort_pages/pallas_call | solution.py:190
  3.1 0.0 copy-start.4
  3.1 0.0 copy-start.2
  3.1 0.0 copy-start.3
  3.1 0.0 copy-start.1
  3.1 7.7 %all-to-all-start = ((bf16[16,8,8,512]{3,2,1,0:T(8,128)(2,1)}), bf16[16,8,8,512]{3,2,1,0:T(8,128)(2,1)S(1)}, u32[]{:S(2)}, u32[]{:S(2)}) async-start(bf16[16,8,8,512]{3,2,1,0:T(8,128)(2,1)} %sort_pages.1), calls=%async_computation | async-start | bytes 2097152 | tf_op jit(solution)/shard_map/all_to_all | solution.py:297
  10.9 0.0 copy-done
  10.9 2.9 %fusion = f32[128,512]{1,0:T(8,128)S(1)} fusion(bf16[4096,512]{1,0:T(8,128)(2,1)} %param.10, bf16[1,128,4096]{2,1,0:T(8,128)(2,1)S(1)} %copy-done), kind=kOutput, calls=%fused_computation.1 | convolution fusion | flops 536870912 | bytes 5505024 | tf_op jit(solution)/shard_map/dot_general | solution.py:300
  13.8 1.0 %collective-permute-start = (f32[128,512]{1,0:T(8,128)S(1)}, f32[128,512]{1,0:T(8,128)S(1)}, u32[]{:S(2)}, u32[]{:S(2)}) collective-permute-start(f32[128,512]{1,0:T(8,128)S(1)} %fusion), channel_id=1, source_target_pairs={{0,1},{1,0},{2,3},{3,2},{4,5},{5,4},{6,7},{7,6},{8,9},{9,8},{10,11... | collective-permute-start | bytes 786440 | tf_op jit(solution)/shard_map/ppermute | solution.py:301
  14.8 0.0 copy-done.4
  14.8 0.0 copy-done.2
  14.9 0.0 copy-done.3
  14.9 0.1 select_reduce_fusion
  15.0 0.1 reshape.118
  15.1 0.6 gather_fusion
  15.7 0.1 multiply_add_fusion
  16.4 0.1 fusion.2
  16.5 0.1 select_n.54.bias_ref
  16.6 0.0 collective-permute-done
  16.6 0.1 multiply_reduce_fusion
  16.8 0.0 copy-done.1
  16.8 0.1 multiply_convert_fusion.refs_0_
  16.9 10.0 %all-to-all-done = bf16[16,8,8,512]{3,2,1,0:T(8,128)(2,1)S(1)} async-done(((bf16[16,8,8,512]{3,2,1,0:T(8,128)(2,1)}), bf16[16,8,8,512]{3,2,1,0:T(8,128)(2,1)S(1)}, u32[]{:S(2)}, u32[]{:S(2)}) %all-to-all-start) | async-done | bytes 1048608 | tf_op jit(solution)/shard_map/all_to_all | solution.py:297
  26.8 0.1 slice_bitcast_fusion.1
  26.9 0.1 pad_maximum_fusion
  27.0 2.7 %collective-permute-start.1 = (bf16[4,16,8,512]{3,2,1,0:T(8,128)(2,1)S(1)}, bf16[4,16,8,512]{3,2,1,0:T(8,128)(2,1)S(1)}, u32[]{:S(2)}, u32[]{:S(2)}) collective-permute-start(bf16[4,16,8,512]{3,2,1,0:T(8,128)(2,1)S(1)} %pad_maximum_fusion), channel_id=1, source_target_pairs={{0,1},{1,0},{2,3},{3,2},{4,5},{5,4},{6,7},{7,6},{8,9},{9,8},{10,11... | collective-permute-start | bytes 1572872 | tf_op jit(solution)/shard_map/ppermute | solution.py:318
  29.7 1.5 %collective-permute-done.1 = bf16[4,16,8,512]{3,2,1,0:T(8,128)(2,1)S(1)} collective-permute-done((bf16[4,16,8,512]{3,2,1,0:T(8,128)(2,1)S(1)}, bf16[4,16,8,512]{3,2,1,0:T(8,128)(2,1)S(1)}, u32[]{:S(2)}, u32[]{:S(2)}) %collective-permute-start.1) | collective-permute-done | bytes 524320 | tf_op jit(solution)/shard_map/ppermute | solution.py:318
  31.3 5.7 %collective-permute-start.3 = (bf16[3,16,8,512]{3,2,1,0:T(8,128)(2,1)S(1)}, bf16[3,16,8,512]{3,2,1,0:T(8,128)(2,1)S(1)}, u32[]{:S(2)}, u32[]{:S(2)}) collective-permute-start(bf16[3,16,8,512]{3,2,1,0:T(8,128)(2,1)S(1)} %pad_maximum_fusion.1), channel_id=1, source_target_pairs={{0,32},{1,225},{2,34},{3,227},{4,36},{5,229},{6,38},{7,231},{8,40}... | collective-permute-start | bytes 1179656 | tf_op jit(solution)/shard_map/ppermute | solution.py:282
  37.0 1.2 %collective-permute-start.2 = (bf16[2,16,8,512]{3,2,1,0:T(8,128)(2,1)S(1)}, bf16[2,16,8,512]{3,2,1,0:T(8,128)(2,1)S(1)}, u32[]{:S(2)}, u32[]{:S(2)}) collective-permute-start(bf16[2,16,8,512]{3,2,1,0:T(8,128)(2,1)S(1)} %pad_maximum_fusion.3), channel_id=1, source_target_pairs={{0,64},{1,193},{2,66},{3,195},{4,68},{5,197},{6,70},{7,199},{8,72}... | collective-permute-start | bytes 786440 | tf_op jit(solution)/shard_map/ppermute | solution.py:282
  38.3 7.3 %attend.4 = (f32[4096,512]{1,0:T(8,128)S(1)}, f32[4096,128]{1,0:T(8,128)S(1)}, f32[4096,128]{1,0:T(8,128)S(1)}, bf16[4096,512]{1,0:T(8,128)(2,1)S(1)}, bf16[64,512]{1,0:T(8,128)(2,1)}, /*index=5*/f32[8,128]{1,0:T(8,128)S(1)}) custom-call(bf16[4096,512]{1,0:T(8,128)(2,1)} %bitcast.43, f32[1,2048]{1,0:T(1,128)S(1)} %select_n.54.bias_ref, ...), custom_call_target="tpu_custom_call" | custom-call | bytes 65536 | tf_op jit(solution)/shard_map/attend/pallas_call | solution.py:208
  45.6 0.0 collective-permute-done.3
  45.6 0.1 collective-permute-start.4
  45.8 1.6 %collective-permute-start.6 = (bf16[3,16,8,512]{3,2,1,0:T(8,128)(2,1)S(1)}, bf16[3,16,8,512]{3,2,1,0:T(8,128)(2,1)S(1)}, u32[]{:S(2)}, u32[]{:S(2)}) collective-permute-start(bf16[3,16,8,512]{3,2,1,0:T(8,128)(2,1)S(1)} %pad_maximum_fusion.2), channel_id=1, source_target_pairs={{0,96},{1,161},{2,98},{3,163},{4,100},{5,165},{6,102},{7,167},{8,1... | collective-permute-start | bytes 1179656 | tf_op jit(solution)/shard_map/ppermute | solution.py:282
  47.4 0.0 collective-permute-done.2
  47.4 1.3 %collective-permute-start.5 = (bf16[2,16,8,512]{3,2,1,0:T(8,128)(2,1)S(1)}, bf16[2,16,8,512]{3,2,1,0:T(8,128)(2,1)S(1)}, u32[]{:S(2)}, u32[]{:S(2)}) collective-permute-start(bf16[2,16,8,512]{3,2,1,0:T(8,128)(2,1)S(1)} %collective-permute-done.2), channel_id=1, source_target_pairs={{0,1},{1,0},{2,3},{3,2},{4,5},{5,4},{6,7},{7,6},{8,9},{9,8},{10,11... | collective-permute-start | bytes 786440 | tf_op jit(solution)/shard_map/ppermute | solution.py:326
  48.7 0.0 collective-permute-done.4
  48.7 5.6 %attend.5 = (f32[4096,512]{1,0:T(8,128)S(1)}, f32[4096,128]{1,0:T(8,128)S(1)}, f32[4096,128]{1,0:T(8,128)S(1)}, f32[8,128]{1,0:T(8,128)S(1)}) custom-call(bf16[4096,512]{1,0:T(8,128)(2,1)S(1)} %get-tuple-element.35.held_ref, f32[1,2048]{1,0:T(1,128)S(1)} %select_n.54.bias_ref, ...), custom_call_target="tpu_custom_call", output_to_operand_aliasing={{0}: (2, {}), {1}: (3, {}), {2}: (4, {})} | custom-call | bytes 65536 | tf_op jit(solution)/shard_map/attend/pallas_call | solution.py:208
  54.3 0.0 collective-permute-done.5
  54.3 5.6 %attend.6 = (f32[4096,512]{1,0:T(8,128)S(1)}, f32[4096,128]{1,0:T(8,128)S(1)}, f32[4096,128]{1,0:T(8,128)S(1)}, f32[8,128]{1,0:T(8,128)S(1)}) custom-call(bf16[4096,512]{1,0:T(8,128)(2,1)S(1)} %get-tuple-element.35.held_ref, f32[1,2048]{1,0:T(1,128)S(1)} %select_n.54.bias_ref, ...), custom_call_target="tpu_custom_call", output_to_operand_aliasing={{0}: (2, {}), {1}: (3, {}), {2}: (4, {})} | custom-call | bytes 65536 | tf_op jit(solution)/shard_map/attend/pallas_call | solution.py:208
  59.9 0.0 collective-permute-done.6
  59.9 5.6 %collective-permute-start.7 = (bf16[3,16,8,512]{3,2,1,0:T(8,128)(2,1)S(1)}, bf16[3,16,8,512]{3,2,1,0:T(8,128)(2,1)S(1)}, u32[]{:S(2)}, u32[]{:S(2)}) collective-permute-start(bf16[3,16,8,512]{3,2,1,0:T(8,128)(2,1)S(1)} %collective-permute-done.6), channel_id=1, source_target_pairs={{0,1},{1,0},{2,3},{3,2},{4,5},{5,4},{6,7},{7,6},{8,9},{9,8},{10,11... | collective-permute-start | bytes 1179656 | tf_op jit(solution)/shard_map/ppermute | solution.py:326
  65.6 1.3 %collective-permute-done.7 = bf16[3,16,8,512]{3,2,1,0:T(8,128)(2,1)S(1)} collective-permute-done((bf16[3,16,8,512]{3,2,1,0:T(8,128)(2,1)S(1)}, bf16[3,16,8,512]{3,2,1,0:T(8,128)(2,1)S(1)}, u32[]{:S(2)}, u32[]{:S(2)}) %collective-permute-start.7) | collective-permute-done | bytes 393248 | tf_op jit(solution)/shard_map/ppermute | solution.py:326
  66.9 9.4 %attend.7 = bf16[4096,512]{1,0:T(8,128)(2,1)} custom-call(bf16[4096,512]{1,0:T(8,128)(2,1)S(1)} %get-tuple-element.35.held_ref, f32[1,2048]{1,0:T(1,128)S(1)} %select_n.54.bias_ref, f32[4096,512]{1,0:T(8,128)S(1)} %get-tuple-element.48.acc_in, f32[4096,128]{1,0:T(8,128)S(1)} %get-tuple-element.49.high_in, f32[4096,128]{1,0:T(8,128)S(1)} %get-tuple-element.50.sum_in, ...), custom_call_target="tpu_custom_call" | custom-call | bytes 65536 | tf_op jit(solution)/shard_map/attend/pallas_call | solution.py:208
  (10 shorter events, 0.2 us)
Async XLA Ops:
  0.6 10.2 %copy-start = (bf16[1,128,4096]{2,1,0:T(8,128)(2,1)S(1)}, bf16[1,128,4096]{2,1,0:T(8,128)(2,1)}, u32[]{:S(2)}) copy-start(bf16[1,128,4096]{2,1,0:T(8,128)(2,1)} %param.9) | copy-start | bytes 3145732
  3.1 11.8 %copy-start.4 = (s32[16]{0:T(128)S(1)}, s32[16]{0:T(128)}, u32[]{:S(2)}) copy-start(s32[16]{0:T(128)} %constant.80.clone) | copy-start | bytes 196
  3.1 11.8 %copy-start.2 = (s32[16]{0:T(128)S(1)}, s32[16]{0:T(128)}, u32[]{:S(2)}) copy-start(s32[16]{0:T(128)} %constant.79.clone) | copy-start | bytes 196
  3.1 11.8 %copy-start.3 = (s32[1,128]{1,0:T(1,128)S(1)}, s32[1,128]{1,0:T(1,128)}, u32[]{:S(2)}) copy-start(s32[1,128]{1,0:T(1,128)} %param.14) | copy-start | bytes 1540
  3.1 13.6 %copy-start.1 = (f32[512]{0:T(512)S(1)}, f32[512]{0:T(512)}, u32[]{:S(2)}) copy-start(f32[512]{0:T(512)} %param.11) | copy-start | bytes 6148
  3.1 23.7 %all-to-all-start = ((bf16[16,8,8,512]{3,2,1,0:T(8,128)(2,1)}), bf16[16,8,8,512]{3,2,1,0:T(8,128)(2,1)S(1)}, u32[]{:S(2)}, u32[]{:S(2)}) async-start(bf16[16,8,8,512]{3,2,1,0:T(8,128)(2,1)} %sort_pages.1), calls=%async_computation | async-start | bytes 2097152 | tf_op jit(solution)/shard_map/all_to_all | solution.py:297
  13.8 2.8 %collective-permute-start = (f32[128,512]{1,0:T(8,128)S(1)}, f32[128,512]{1,0:T(8,128)S(1)}, u32[]{:S(2)}, u32[]{:S(2)}) collective-permute-start(f32[128,512]{1,0:T(8,128)S(1)} %fusion), channel_id=1, source_target_pairs={{0,1},{1,0},{2,3},{3,2},{4,5},{5,4},{6,7},{7,6},{8,9},{9,8},{10,11... | collective-permute-start | bytes 786440 | tf_op jit(solution)/shard_map/ppermute | solution.py:301
  27.0 4.2 %collective-permute-start.1 = (bf16[4,16,8,512]{3,2,1,0:T(8,128)(2,1)S(1)}, bf16[4,16,8,512]{3,2,1,0:T(8,128)(2,1)S(1)}, u32[]{:S(2)}, u32[]{:S(2)}) collective-permute-start(bf16[4,16,8,512]{3,2,1,0:T(8,128)(2,1)S(1)} %pad_maximum_fusion), channel_id=1, source_target_pairs={{0,1},{1,0},{2,3},{3,2},{4,5},{5,4},{6,7},{7,6},{8,9},{9,8},{10,11... | collective-permute-start | bytes 1572872 | tf_op jit(solution)/shard_map/ppermute | solution.py:318
  31.3 14.3 %collective-permute-start.3 = (bf16[3,16,8,512]{3,2,1,0:T(8,128)(2,1)S(1)}, bf16[3,16,8,512]{3,2,1,0:T(8,128)(2,1)S(1)}, u32[]{:S(2)}, u32[]{:S(2)}) collective-permute-start(bf16[3,16,8,512]{3,2,1,0:T(8,128)(2,1)S(1)} %pad_maximum_fusion.1), channel_id=1, source_target_pairs={{0,32},{1,225},{2,34},{3,227},{4,36},{5,229},{6,38},{7,231},{8,40}... | collective-permute-start | bytes 1179656 | tf_op jit(solution)/shard_map/ppermute | solution.py:282
  37.0 10.4 %collective-permute-start.2 = (bf16[2,16,8,512]{3,2,1,0:T(8,128)(2,1)S(1)}, bf16[2,16,8,512]{3,2,1,0:T(8,128)(2,1)S(1)}, u32[]{:S(2)}, u32[]{:S(2)}) collective-permute-start(bf16[2,16,8,512]{3,2,1,0:T(8,128)(2,1)S(1)} %pad_maximum_fusion.3), channel_id=1, source_target_pairs={{0,64},{1,193},{2,66},{3,195},{4,68},{5,197},{6,70},{7,199},{8,72}... | collective-permute-start | bytes 786440 | tf_op jit(solution)/shard_map/ppermute | solution.py:282
  45.6 3.1 %collective-permute-start.4 = (bf16[3,16,8,512]{3,2,1,0:T(8,128)(2,1)S(1)}, bf16[3,16,8,512]{3,2,1,0:T(8,128)(2,1)S(1)}, u32[]{:S(2)}, u32[]{:S(2)}) collective-permute-start(bf16[3,16,8,512]{3,2,1,0:T(8,128)(2,1)S(1)} %collective-permute-done.3), channel_id=1, source_target_pairs={{0,1},{1,0},{2,3},{3,2},{4,5},{5,4},{6,7},{7,6},{8,9},{9,8},{10,11... | collective-permute-start | bytes 1179656 | tf_op jit(solution)/shard_map/ppermute | solution.py:326
  45.8 14.1 %collective-permute-start.6 = (bf16[3,16,8,512]{3,2,1,0:T(8,128)(2,1)S(1)}, bf16[3,16,8,512]{3,2,1,0:T(8,128)(2,1)S(1)}, u32[]{:S(2)}, u32[]{:S(2)}) collective-permute-start(bf16[3,16,8,512]{3,2,1,0:T(8,128)(2,1)S(1)} %pad_maximum_fusion.2), channel_id=1, source_target_pairs={{0,96},{1,161},{2,98},{3,163},{4,100},{5,165},{6,102},{7,167},{8,1... | collective-permute-start | bytes 1179656 | tf_op jit(solution)/shard_map/ppermute | solution.py:282
  47.4 6.9 %collective-permute-start.5 = (bf16[2,16,8,512]{3,2,1,0:T(8,128)(2,1)S(1)}, bf16[2,16,8,512]{3,2,1,0:T(8,128)(2,1)S(1)}, u32[]{:S(2)}, u32[]{:S(2)}) collective-permute-start(bf16[2,16,8,512]{3,2,1,0:T(8,128)(2,1)S(1)} %collective-permute-done.2), channel_id=1, source_target_pairs={{0,1},{1,0},{2,3},{3,2},{4,5},{5,4},{6,7},{7,6},{8,9},{9,8},{10,11... | collective-permute-start | bytes 786440 | tf_op jit(solution)/shard_map/ppermute | solution.py:326
  59.9 7.0 %collective-permute-start.7 = (bf16[3,16,8,512]{3,2,1,0:T(8,128)(2,1)S(1)}, bf16[3,16,8,512]{3,2,1,0:T(8,128)(2,1)S(1)}, u32[]{:S(2)}, u32[]{:S(2)}) collective-permute-start(bf16[3,16,8,512]{3,2,1,0:T(8,128)(2,1)S(1)} %collective-permute-done.6), channel_id=1, source_target_pairs={{0,1},{1,0},{2,3},{3,2},{4,5},{5,4},{6,7},{7,6},{8,9},{9,8},{10,11... | collective-permute-start | bytes 1179656 | tf_op jit(solution)/shard_map/ppermute | solution.py:326
